TPU v7x, 256 devices: a whole 4x4x8 slice. The times are simulated.
256 devices in a mesh: dp: 16 (over z, core), ctx: 16 (over y, x).
Axes of the slice: x: 4, y: 4, z: 8, core: 2. Of those that a mesh axis runs over, the one named last changes fastest.
Arguments:
- queries_in: bfloat16 [16, 16, 128, 2048], P('dp', None, 'ctx'), may hold values from -100 to 100
- keys_in: bfloat16 [16, 16, 128, 2048], P('dp', None, 'ctx'), may hold values from -4 to 4
- values_in: bfloat16 [16, 16, 128, 2048], P('dp', None, 'ctx'), may hold values from -6 to 6
- upstream: bfloat16 [16, 2048, 2048], P('dp', 'ctx'), may hold values from -6 to 6
- lengths: int32 [16], replicated, may hold values from 256 to 2048, as said below
- assignment: int32 [16], replicated, may hold values from 0 to 15, each once
- span_order: int32 [16, 256], replicated, may hold values from 0 to 255, as said below
Outputs:
- attended: bfloat16 [16, 2048, 2048], P('dp', 'ctx')
- query_grad: bfloat16 [16, 2048, 2048], P('dp', 'ctx')
- key_grad: bfloat16 [16, 2048, 2048], P('dp', 'ctx')
- value_grad: bfloat16 [16, 2048, 2048], P('dp', 'ctx')
Inputs may be any that keep to these rules, and one draw needn't show every extreme that they name: `lengths`: one episode has exactly 2048 tokens. `span_order`: for each episode one of two layouts is drawn: span s * 16 + c sits at block c * 16 + s, or at block c * 8 + s for s < 8 and at (31 - c) * 8 + s - 8 otherwise.
All inputs are finite; a program needn't handle non-finite values.
Results may differ from a plain program's by a relative error of at most 0.03.
Values may be sent and summed in bfloat16 or wider, within the bound.
A program may use at most 192 MiB of HBM per device.

v0:
```python
import math

import jax
import jax.numpy as jnp
from jax import lax
from jax.sharding import PartitionSpec as P

HEADS = 16
HEAD_DIM = 128


masked_value = -1e30


def per_device(queries_in, keys_in, values_in, upstream, lengths, assignment, span_order):
    ctx_size = lax.axis_size("ctx")
    dp_size = lax.axis_size("dp")
    shard = lax.axis_index("dp")
    column = lax.axis_index("ctx")
    scaling = 1.0 / math.sqrt(HEAD_DIM)
    episodes = assignment.shape[0]
    labels = jnp.arange(episodes, dtype=jnp.int32)
    sources = jnp.sum(jnp.where(assignment[None, :] == labels[:, None], labels[None, :], 0), axis=1)
    episode = sources[shard]
    queries, keys, values = (
        lax.all_to_all(
            jnp.take(queries_in[0], sources, axis=0), "dp", split_axis=0, concat_axis=0, tiled=True
        ),
        lax.all_to_all(
            jnp.take(keys_in[0], sources, axis=0), "dp", split_axis=0, concat_axis=0, tiled=True
        ),
        lax.all_to_all(
            jnp.take(values_in[0], sources, axis=0), "dp", split_axis=0, concat_axis=0, tiled=True
        ),
    )
    span_rows = queries.shape[1]
    row_count = queries.shape[0] * span_rows
    queries = queries.reshape(row_count, HEADS, HEAD_DIM)
    keys = keys.reshape(row_count, HEADS, HEAD_DIM)
    values = values.reshape(row_count, HEADS, HEAD_DIM)
    length = lengths[episode]
    layout = lax.dynamic_index_in_dim(span_order, episode, 0, keepdims=False).reshape(
        dp_size, ctx_size
    )
    places = (layout.T[:, :, None] * span_rows + jnp.arange(span_rows, dtype=jnp.int32)).reshape(
        ctx_size * row_count
    )
    own_places = lax.dynamic_slice_in_dim(places, column * row_count, row_count)
    alive = own_places < length
    keys_all, values_all = (
        lax.all_gather(keys, "ctx", axis=0, tiled=True),
        lax.all_gather(values, "ctx", axis=0, tiled=True),
    )
    scores = (
        jnp.einsum("qhd,khd->hqk", queries, keys_all, preferred_element_type=jnp.float32) * scaling
    )
    visible = (places[None, :] <= own_places[:, None]) & (places < length)[None, :]
    scores = jnp.where(visible[None], scores, masked_value)
    peak = jnp.max(scores, axis=2)
    weights = jnp.exp(scores - peak[:, :, None])
    totals = jnp.sum(weights, axis=2)
    blended = (
        jnp.einsum(
            "hqk,khd->qhd",
            weights.astype(jnp.bfloat16),
            values_all,
            preferred_element_type=jnp.float32,
        )
        / totals.T[:, :, None]
    )
    attended = jnp.where(alive[:, None, None], blended, 0.0).astype(jnp.bfloat16)
    log_total = (peak + jnp.log(totals)).T
    given = upstream[0].reshape(row_count, HEADS, HEAD_DIM)
    incoming = jnp.where(alive[:, None, None], given, jnp.zeros_like(given))
    row_dots = jnp.sum(incoming.astype(jnp.float32) * attended.astype(jnp.float32), axis=2)

    def query_block(block):
        block_scores = lax.dynamic_slice_in_dim(scores, block * row_count, row_count, 2)
        block_keys = lax.dynamic_slice_in_dim(keys_all, block * row_count, row_count, 0)
        block_values = lax.dynamic_slice_in_dim(values_all, block * row_count, row_count, 0)
        probs = jnp.exp(block_scores - log_total.T[:, :, None])
        dweights = jnp.einsum(
            "qhd,khd->hqk", incoming, block_values, preferred_element_type=jnp.float32
        )
        dscores = (probs * (dweights - row_dots.T[:, :, None])).astype(jnp.bfloat16)
        return jnp.einsum("hqk,khd->qhd", dscores, block_keys, preferred_element_type=jnp.float32)

    def add_block(block, query_sum):
        term = query_block(block)
        return query_sum + term

    start_sum = jnp.zeros((row_count, HEADS, HEAD_DIM), jnp.float32)
    query_sum = lax.fori_loop(0, ctx_size, add_block, start_sum)
    totals_all, dots_all = (
        lax.all_gather(log_total, "ctx", axis=0, tiled=True),
        lax.all_gather(row_dots, "ctx", axis=0, tiled=True),
    )
    query_piece = lax.all_gather(queries, "ctx", axis=0, tiled=True)
    incoming_piece = lax.all_gather(incoming, "ctx", axis=0, tiled=True)
    allowed = (own_places[None, :] <= places[:, None]) & alive[None, :] & (places < length)[:, None]
    piece_scores = (
        jnp.einsum("qhd,khd->hqk", query_piece, keys, preferred_element_type=jnp.float32) * scaling
    )
    piece_scores = jnp.where(allowed[None], piece_scores, masked_value)
    probs = jnp.exp(piece_scores - totals_all.T[:, :, None])
    dweights = jnp.einsum(
        "qhd,khd->hqk", incoming_piece, values, preferred_element_type=jnp.float32
    )
    dscores = probs * (dweights - dots_all.T[:, :, None])
    value_sum = jnp.einsum(
        "hqk,qhd->khd",
        probs.astype(jnp.bfloat16),
        incoming_piece,
        preferred_element_type=jnp.float32,
    )
    key_sum = jnp.einsum(
        "hqk,qhd->khd",
        dscores.astype(jnp.bfloat16),
        query_piece,
        preferred_element_type=jnp.float32,
    )
    key_sum, value_sum = (key_sum, value_sum)
    feat = HEADS * HEAD_DIM
    return (
        attended.reshape(1, row_count, feat),
        (query_sum * scaling).astype(jnp.bfloat16).reshape(1, row_count, feat),
        (key_sum * scaling).astype(jnp.bfloat16).reshape(1, row_count, feat),
        value_sum.astype(jnp.bfloat16).reshape(1, row_count, feat),
    )


def solution(mesh):
    in_specs = (
        P("dp", None, "ctx", None),
        P("dp", None, "ctx", None),
        P("dp", None, "ctx", None),
        P("dp", "ctx", None),
        P(),
        P(),
        P(),
    )
    out_specs = (
        P("dp", "ctx", None),
        P("dp", "ctx", None),
        P("dp", "ctx", None),
        P("dp", "ctx", None),
    )
    return jax.shard_map(
        per_device, mesh=mesh, in_specs=in_specs, out_specs=out_specs, check_vma=False
    )
```

profile of v0, /device:TPU:1, one launch (start us, length us, event | category | flops | bytes accessed | tf_op | source)
XLA Modules:
  0.0 402.9 jit_solution(4996412942729544843)
XLA Ops:
  8.8 1.6 gather_fusion.2
  10.4 1.6 gather_fusion
  12.3 27.1 %all_to_all.15 = bf16[16,8,2048]{2,1,0:T(8,128)(2,1)S(1)} all-to-all(bf16[16,8,2048]{2,1,0:T(8,128)(2,1)S(1)} %get-tuple-element.229), channel_id=1, replica_groups=mesh['dp'=16,'ctx'=16] {'dp'}, dimensions={0} | all-to-all | bytes 1048576 | tf_op jit(solution)/shard_map/all_to_all | solution.py:29
  40.5 20.0 %all_to_all.16 = bf16[16,8,2048]{2,1,0:T(8,128)(2,1)S(1)} all-to-all(bf16[16,8,2048]{2,1,0:T(8,128)(2,1)S(1)} %get-tuple-element.230), channel_id=1, replica_groups=mesh['dp'=16,'ctx'=16] {'dp'}, dimensions={0} | all-to-all | bytes 1048576 | tf_op jit(solution)/shard_map/all_to_all | solution.py:32
  62.0 20.0 %all_to_all.17 = bf16[16,8,2048]{2,1,0:T(8,128)(2,1)S(1)} all-to-all(bf16[16,8,2048]{2,1,0:T(8,128)(2,1)S(1)} %get-tuple-element.228), channel_id=1, replica_groups=mesh['dp'=16,'ctx'=16] {'dp'}, dimensions={0} | all-to-all | bytes 1048576 | tf_op jit(solution)/shard_map/all_to_all | solution.py:26
  85.2 1.3 copy.42
  90.5 22.6 %all-gather.7.cloned.1.call-done = bf16[2048,16,128]{2,0,1:T(8,128)(2,1)} async-done(((bf16[128,16,128]{2,0,1:T(8,128)(2,1)}), bf16[2048,16,128]{2,0,1:T(8,128)(2,1)}) %all-gather.7.cloned.1.call-update) | async-done | bytes 8388624 | tf_op jit(solution)/shard_map/all_gather | solution.py:51
  113.1 12.4 %fusion.46 = (f32[16,128]{1,0:T(8,128)S(1)}, f32[16,128,2048]{2,1,0:T(8,128)}) fusion(bf16[2048,16,128]{2,0,1:T(8,128)(2,1)} %all-gather.7.cloned.1.call-done, bf16[128,16,128]{2,1,0:T(8,128)(2,1)S(1)} %bitcast.75, pred[128,2048]{1,0:T(8,128)(4,1)S(1)} %compare_and_fusion), kind=kOutput, calls=%fused_computation.65 | convolution fusion | flops 1086322688 | bytes 25960448 | tf_op jit(solution)/shard_map/qhd,khd->hqk/dot_general | solution.py:55
  125.5 8.7 %fusion.13 = f32[16,128]{1,0:T(8,128)S(1)} fusion(f32[16,128,2048]{2,1,0:T(8,128)} %get-tuple-element.286, f32[16,128]{1,0:T(8,128)S(1)} %get-tuple-element.231), kind=kLoop, calls=%fused_computation.21 | loop fusion | flops 8386560 | bytes 16793600 | tf_op jit(solution)/shard_map/reduce_sum | solution.py:61
  134.2 64.1 %all-gather.5.cloned.1.call-done = bf16[2048,16,128]{0,2,1:T(8,128)(2,1)} async-done(((bf16[128,16,128]{0,2,1:T(8,128)(2,1)}), bf16[2048,16,128]{0,2,1:T(8,128)(2,1)}) %all-gather.5.cloned.1.call-update) | async-done | bytes 8388624 | tf_op jit(solution)/shard_map/all_gather | solution.py:52
  198.3 11.9 %multiply_reduce_fusion = (f32[128,16]{0,1:T(8,128)S(1)}, bf16[128,16,128]{0,2,1:T(8,128)(2,1)}, bf16[128,16,128]{0,2,1:T(8,128)(2,1)S(1)}) fusion(bf16[128,16,128]{0,2,1:T(8,128)(2,1)S(1)} %bitcast.82, pred[128]{0:T(512)(128)(4,1)S(1)} %get-tuple-element.226, f32[128,16]{0,1:T(8,128)S(1)} %bitcast.91, ...), kind=kOutput, calls=%fused_computation.39 | convolution fusion | flops 1084225536 | bytes 26763392 | tf_op jit(solution)/shard_map/hqk,khd->qhd/dot_general | solution.py:63
  210.2 1.5 and_and_fusion
  211.7 1.3 copy.46
  214.1 78.7 %while.14 = (s32[]{:T(128)}, f32[128,16,128]{0,2,1:T(8,128)}, bf16[2048,16,128]{2,0,1:T(8,128)(2,1)}, f32[16,128,2048]{2,1,0:T(8,128)}, f32[16,128]{1,0:T(8,128)...) while((s32[]{:T(128)}, f32[128,16,128]{0,2,1:T(8,128)}, ...), condition=%wide.region_5.7_spmd.clone, body=%wide.region_4.6_spmd.clone.sunk | while | flops 135790592 | bytes 8931000 | solution.py:93
  214.1 1.3 constant_dynamic-slice_fusion.2
  215.7 2.9 fusion.70
  218.6 1.3 constant_dynamic-slice_fusion.2
  220.3 3.3 fusion.70
  223.6 1.3 constant_dynamic-slice_fusion.2
  225.2 3.3 fusion.70
  228.5 1.3 constant_dynamic-slice_fusion.2
  230.2 3.3 fusion.70
  233.4 1.3 constant_dynamic-slice_fusion.2
  235.1 3.3 fusion.70
  238.3 1.3 constant_dynamic-slice_fusion.2
  240.0 3.5 fusion.70
  243.5 1.3 constant_dynamic-slice_fusion.2
  245.1 3.3 fusion.70
  248.4 1.3 constant_dynamic-slice_fusion.2
  250.0 3.3 fusion.70
  254.9 3.3 fusion.70
  258.3 1.3 constant_dynamic-slice_fusion.2
  260.0 3.3 fusion.70
  263.3 1.3 constant_dynamic-slice_fusion.2
  265.0 3.3 fusion.70
  269.9 3.3 fusion.70
  274.8 3.3 fusion.70
  279.7 3.3 fusion.70
  284.6 3.3 fusion.70
  289.5 3.3 fusion.70
  292.7 1.4 multiply_convert_fusion.6
  295.2 18.6 %all_gather.23 = f32[2048,16]{0,1:T(8,128)S(1)} all-gather(f32[128,16]{0,1:T(8,128)S(1)} %get-tuple-element.334), channel_id=1, replica_groups=mesh['dp'=16,'ctx'=16] {'ctx'}, dimensions={0}, use_global_device_ids=true | all-gather | bytes 139264 | tf_op jit(solution)/shard_map/all_gather | solution.py:96
  313.8 18.1 %all_gather.21 = f32[2048,16]{0,1:T(8,128)S(1)} all-gather(f32[128,16]{0,1:T(8,128)S(1)} %bitcast_add_fusion), channel_id=1, replica_groups=mesh['dp'=16,'ctx'=16] {'ctx'}, dimensions={0}, use_global_device_ids=true | all-gather | bytes 139264 | tf_op jit(solution)/shard_map/all_gather | solution.py:95
  331.9 11.8 %fusion.44 = f32[16,2048,128]{2,1,0:T(8,128)} fusion(bf16[2048,16,128]{2,0,1:T(8,128)(2,1)} %all-gather.9.cloned.1.call-done, bf16[128,16,128]{2,1,0:T(8,128)(2,1)S(1)} %bitcast.73), kind=kOutput, calls=%fused_computation.63 | convolution fusion | flops 1073741824 | bytes 25690112 | tf_op jit(solution)/shard_map/qhd,khd->hqk/dot_general | solution.py:102
  343.7 18.7 %all-gather.11.cloned.1.call-done = bf16[2048,16,128]{0,2,1:T(8,128)(2,1)} async-done(((bf16[128,16,128]{0,2,1:T(8,128)(2,1)}), bf16[2048,16,128]{0,2,1:T(8,128)(2,1)}) %all-gather.11.cloned.1.call-update) | async-done | bytes 8388624 | tf_op jit(solution)/shard_map/all_gather | solution.py:99
  362.4 15.0 %multiply_convert_fusion.9 = bf16[16,2048,128]{2,1,0:T(8,128)(2,1)} fusion(f32[16,2048,128]{2,1,0:T(8,128)} %fusion.44, f32[16,2048]{1,0:T(8,128)S(1)} %bitcast.90, f32[16,2048]{1,0:T(8,128)S(1)} %bitcast.88, pred[2048,128]{1,0:T(8,128)(4,1)S(1)} %and_and_fusion, ...), kind=kOutput, calls=%fused_computation.17.clone.clone.clone.clone.clone.clone.1 | convolution fusion | flops 1098907648 | bytes 34603008 | tf_op jit(solution)/shard_map/qhd,khd->hqk/dot_general | solution.py:106
  377.4 6.1 %fusion.36 = bf16[16,128,128]{2,1,0:T(8,128)(2,1)S(1)} fusion(bf16[2048,16,128]{2,0,1:T(8,128)(2,1)S(1)} %copy-done.2, bf16[16,2048,128]{2,1,0:T(8,128)(2,1)} %multiply_convert_fusion.9), kind=kOutput, calls=%fused_computation.37 | convolution fusion | flops 1074266112 | bytes 17301504 | tf_op jit(solution)/shard_map/hqk,qhd->khd/dot_general | solution.py:116
  384.5 10.9 %fusion.33 = bf16[16,128,128]{2,1,0:T(8,128)(2,1)S(1)} fusion(bf16[2048,16,128]{0,2,1:T(8,128)(2,1)} %all-gather.11.cloned.1.call-done, f32[16,2048,128]{2,1,0:T(8,128)} %fusion.44, f32[16,2048]{1,0:T(8,128)S(1)} %bitcast.89, pred[2048,128]{1,0:T(8,128)(4,1)S(1)} %and_and_fusion), kind=kOutput, calls=%fused_computation.36 | convolution fusion | flops 1090781184 | bytes 26083328 | tf_op jit(solution)/shard_map/hqk,qhd->khd/dot_general | solution.py:110
  (70 shorter events, 26.6 us)
Async XLA Ops:
  7.2 1.1 copy-start
  7.2 80.0 %copy-start.4 = (s32[16]{0:T(128)S(1)}, s32[16]{0:T(128)}, u32[]{:S(2)}) copy-start(s32[16]{0:T(128)} %param.15) | copy-start | bytes 196
  7.2 105.9 %all-gather.7.cloned.1.call-start = ((), (), s32[]{:S(2)}) async-start(), calls=%async_computation.4 | async-start | bytes 8912896 | tf_op jit(solution)/shard_map/all_gather | solution.py:51
  40.5 157.9 %all-gather.5.cloned.1.call-start = ((), (), s32[]{:S(2)}) async-start(), calls=%async_computation.3 | async-start | bytes 8912896 | tf_op jit(solution)/shard_map/all_gather | solution.py:52
  61.9 270.0 %all-gather.9.cloned.1.call-start = ((), (), s32[]{:S(2)}) async-start(), calls=%async_computation.5 | async-start | bytes 8912896 | tf_op jit(solution)/shard_map/all_gather | solution.py:98
  83.1 279.3 %all-gather.11.cloned.1.call-start = ((), (), s32[]{:S(2)}) async-start(), calls=%async_computation.6 | async-start | bytes 8912896 | tf_op jit(solution)/shard_map/all_gather | solution.py:99
  331.9 30.5 %copy-start.3 = (bf16[128,16,128]{0,2,1:T(8,128)(2,1)S(1)}, bf16[128,16,128]{0,2,1:T(8,128)(2,1)}, u32[]{:S(2)}) copy-start(bf16[128,16,128]{0,2,1:T(8,128)(2,1)} %copy.39) | copy-start | bytes 1572868
  362.4 15.0 %copy-start.2 = (bf16[2048,16,128]{2,0,1:T(8,128)(2,1)S(1)}, bf16[2048,16,128]{2,0,1:T(8,128)(2,1)}, u32[]{:S(2)}) copy-start(bf16[2048,16,128]{2,0,1:T(8,128)(2,1)} %all-gather.9.cloned.1.call-done) | copy-start | bytes 25165828
  383.5 12.9 %copy-start.1 = (bf16[1,16,8,2048]{3,2,1,0:T(8,128)(2,1)S(1)}, bf16[1,16,8,2048]{3,2,1,0:T(8,128)(2,1)}, u32[]{:S(2)}) copy-start(bf16[1,16,8,2048]{3,2,1,0:T(8,128)(2,1)} %param.11) | copy-start | bytes 1572868
Sparse Core Ops, SparseCore 0:
  40.6 72.4 all-gather.6
  116.1 82.2 all-gather.4
  200.8 76.0 all-gather.8
  279.7 82.6 all-gather.10
where the time goes:
time: 405 us; the launch traced here: 403 us
  matrix products  120 us (30%)
  waiting for transfers between devices  106 us (26%)
  blocking collectives  104 us (26%)
  local copies, waits for them, and re-layouts  41.7 us (10%)
  between operations  15.9 us (4%)
  other arithmetic  15 us (4%)
    all_gather x1, waiting for transfers between devices, per_device(): lax.all_gather(values, 'ctx', axis=0, tiled=True)  64.1 us
    dot_general x16, matrix products, query_block(): jnp.einsum('hqk,khd->qhd', dscores, block_keys, preferred_element_type=jn...  52.2 us
    all_to_all x1, blocking collectives, per_device(): lax.all_to_all(jnp.take(keys_in[0], sources, axis=0), 'dp', split_axis=0,...  27.1 us
    dynamic_slice x32, local copies, waits for them, and re-layouts, query_block(): lax.dynamic_slice_in_dim(scores, block * row_count, row_count, 2)  26.1 us
    all_gather x1, waiting for transfers between devices, per_device(): lax.all_gather(keys, 'ctx', axis=0, tiled=True)  22.6 us
    all_to_all x1, blocking collectives, per_device(): lax.all_to_all(jnp.take(values_in[0], sources, axis=0), 'dp', split_axis=...  20 us
    all_to_all x1, blocking collectives, per_device(): lax.all_to_all(jnp.take(queries_in[0], sources, axis=0), 'dp', split_axis...  20 us
    all_gather x1, waiting for transfers between devices, per_device(): incoming_piece = lax.all_gather(incoming, 'ctx', axis=0, tiled=True)  18.7 us
  transfers between devices with their start and end apart: 4, of which 3 were waited for; matrix products, arithmetic and copies ran while one was open for 34% of the time, Pallas kernels for 0%

commit v1 on v0

v1 whole, which is shorter than its diff:
```python
import math

import jax
import jax.numpy as jnp
from jax import lax
from jax.experimental import pallas as pl
from jax.experimental.pallas import tpu as pltpu
from jax.sharding import PartitionSpec as P

MESH = pl.DeviceIdType.MESH
N = 16
DIM = 128
ROWS = 128
LEN = 2048
FEAT = 2048
SPAN = 8
CHUNK = 64
BLOCK = 512
SCALE = 1.0 / math.sqrt(DIM)
LOG2E = math.log2(math.e)
MASKED = -1e30
ROWS_BY_ROWS = (((1,), (1,)), ((), ()))
ROWS_BY_COLUMNS = (((1,), (0,)), ((), ()))


def dot(left, right, dims):
    return lax.dot_general(left, right, dims, preferred_element_type=jnp.float32)


def partner(me, i):
    step = jnp.where(i % 2 == 1, (i + 1) // 2, N - i // 2)
    return lax.rem(me + step, N)


def kernel(
    assignment, lengths, span_order, keys_in, queries_in, values_in, upstream,
    attended, query_grad, key_grad, value_grad,
    sources, held_k, held_q, held_v, staged, landed, regrouped, arrived_k, arrived_q, arrived_v, arrived_g,
    ordered, weights, inverse,
    key_sum, value_sum, results, leaving,
    held_sem, up_sem, send_one, recv_one, send_two, recv_two, send_out, recv_out, own_sem,
):
    shard = lax.axis_index("dp")
    column = lax.axis_index("ctx")
    ins = (keys_in, queries_in, values_in)
    outs = (attended, query_grad, key_grad, value_grad)
    held = (held_k, held_q, held_v)
    arrived = (arrived_k, arrived_q, arrived_v, arrived_g)

    loads = [pltpu.make_async_copy(ins[a], held[a], held_sem.at[a]) for a in range(3)]
    for load in loads:
        load.start()

    barrier = pltpu.get_barrier_semaphore()

    def greet(k, carry):
        pl.semaphore_signal(barrier, inc=1, device_id=(lax.rem(shard + k, N), column), device_id_type=MESH)
        pl.semaphore_signal(barrier, inc=1, device_id=(shard, lax.rem(column + k, N)), device_id_type=MESH)
        return carry

    lax.fori_loop(1, N, greet, 0)

    def find(d, carry):
        found = jnp.int32(0)
        for e in range(N):
            found = found + e * (assignment[e] == d).astype(jnp.int32)
        sources[d] = jnp.minimum(found, N - 1)
        return carry

    lax.fori_loop(0, N, find, 0)
    episode = sources[shard]
    length = lengths[episode]
    folded = jnp.clip(2 - lax.div(span_order[episode, 1], SPAN), 0, 1)
    pl.semaphore_wait(barrier, 2 * (N - 1))

    def send_upstream(i, carry):
        to = partner(column, i)
        pltpu.make_async_remote_copy(
            src_ref=upstream.at[:, :, pl.ds(pl.multiple_of(to * DIM, DIM), DIM)],
            dst_ref=arrived[3].at[column],
            send_sem=send_two.at[3],
            recv_sem=recv_two.at[3],
            device_id=(shard, to),
            device_id_type=MESH,
        ).start()
        return carry

    lax.fori_loop(1, N, send_upstream, 0)
    own_up = pltpu.make_async_copy(
        upstream.at[:, :, pl.ds(pl.multiple_of(column * DIM, DIM), DIM)], arrived[3].at[column], up_sem
    )
    own_up.start()

    def by_head(a, to):
        e = sources[to]
        pair = held[a][lax.div(e, 2)].astype(jnp.float32)
        odd = jnp.full((SPAN, FEAT), lax.rem(e, 2), jnp.int32) == 1
        rows = jnp.where(odd, pair[SPAN:], pair[:SPAN])
        heads = [rows[:, h * DIM : (h + 1) * DIM] for h in range(N)]
        return jnp.concatenate(heads, axis=0).astype(jnp.bfloat16)

    def first(a):
        loads[a].wait()

        def send(i, carry):
            to = partner(shard, i)
            staged[a, to] = by_head(a, to)
            pltpu.make_async_remote_copy(
                src_ref=staged.at[a, to],
                dst_ref=landed.at[a, shard],
                send_sem=send_one.at[a],
                recv_sem=recv_one.at[a],
                device_id=(to, column),
                device_id_type=MESH,
            ).start()
            return carry

        lax.fori_loop(1, N, send, 0)
        landed[a, shard] = by_head(a, shard)

    def wait_all(buffer, send_sem, recv_sem):
        whole = pltpu.make_async_remote_copy(
            src_ref=buffer,
            dst_ref=buffer,
            send_sem=send_sem,
            recv_sem=recv_sem,
            device_id=(shard, column),
            device_id_type=MESH,
        )
        whole.wait_recv()
        whole.wait_send()

    def second(a):
        wait_all(landed.at[a, pl.ds(0, N - 1)], send_one.at[a], recv_one.at[a])

        def regroup(pair, carry):
            both = landed[a, :, pl.ds(pl.multiple_of(pair * 16, 16), 16), :].astype(jnp.float32)
            regrouped[a, 2 * pair] = both[:, :SPAN].reshape(2, CHUNK, DIM).astype(jnp.bfloat16)
            regrouped[a, 2 * pair + 1] = both[:, SPAN:].reshape(2, CHUNK, DIM).astype(jnp.bfloat16)
            return carry

        lax.fori_loop(0, N // 2, regroup, 0)

        def send(i, carry):
            to = partner(column, i)
            pltpu.make_async_remote_copy(
                src_ref=regrouped.at[a, to],
                dst_ref=arrived[a].at[column],
                send_sem=send_two.at[a],
                recv_sem=recv_two.at[a],
                device_id=(shard, to),
                device_id_type=MESH,
            ).start()
            return carry

        lax.fori_loop(1, N, send, 0)
        arrived[a][column] = regrouped[a, column]

    def order(a):
        wait_all(arrived[a].at[pl.ds(0, N - 1)], send_two.at[a], recv_two.at[a])

        def place(p, carry):
            second_half = p // N
            piece = p // 2 + folded * (p + second_half * (2 * N - 1 - 2 * p) - p // 2)
            half = p % 2 + folded * (second_half - p % 2)
            ordered[a, pl.ds(pl.multiple_of(p * CHUNK, CHUNK), CHUNK), :] = arrived[a][piece, half]
            return carry

        lax.fori_loop(0, 2 * N, place, 0)

    def give(a):
        def send(i, carry):
            to = partner(column, i)
            low = 2 * to - folded * to
            high = 2 * to + 1 + folded * (2 * N - 2 - 3 * to)
            leaving[a, to, :CHUNK] = results[a, low]
            leaving[a, to, CHUNK:] = results[a, high]
            return carry

        lax.fori_loop(0, N, send, 0)
        own_columns = pl.ds(pl.multiple_of(column * DIM, DIM), DIM)

        def start(i, carry):
            to = partner(column, i)
            pltpu.make_async_remote_copy(
                src_ref=leaving.at[a, to],
                dst_ref=outs[a].at[:, own_columns],
                send_sem=send_out.at[a],
                recv_sem=recv_out.at[a],
                device_id=(shard, to),
                device_id_type=MESH,
            ).start()
            return carry

        lax.fori_loop(1, N, start, 0)
        own = pltpu.make_async_copy(leaving.at[a, column], outs[a].at[:, own_columns], own_sem.at[a])
        own.start()
        return own

    first(0)
    first(1)
    first(2)
    second(0)
    second(1)
    own_up.wait()
    order(3)
    order(0)
    order(1)

    keys, queries, values, given = (ordered.at[a] for a in range(4))
    blocks = LEN // BLOCK
    for b in range(blocks):
        start, stop = b * BLOCK, (b + 1) * BLOCK
        scores = dot(queries[start:stop], keys[:stop], ROWS_BY_ROWS)
        row = lax.broadcasted_iota(jnp.int32, (BLOCK, BLOCK), 0)
        col = lax.broadcasted_iota(jnp.int32, (BLOCK, BLOCK), 1)
        last = jnp.where(col <= row, scores[:, start:], MASKED)
        scores = jnp.concatenate([scores[:, :start], last], axis=1) if b else last
        peak = jnp.max(scores, axis=1, keepdims=True)
        block_weights = jnp.exp2((scores - peak) * (SCALE * LOG2E))
        inverse[start:stop] = 1.0 / jnp.sum(block_weights, axis=1, keepdims=True)
        weights[start:stop, :stop] = block_weights.astype(jnp.bfloat16)

    second(2)
    order(2)

    def chunks(b):
        return slice(b * (BLOCK // CHUNK), (b + 1) * (BLOCK // CHUNK))

    def keep(a, b, rows):
        results[a, chunks(b)] = rows.astype(jnp.bfloat16).reshape(BLOCK // CHUNK, CHUNK, DIM)

    def alive(start):
        return start + lax.broadcasted_iota(jnp.int32, (BLOCK, 1), 0) < length

    for b in range(blocks):
        start, stop = b * BLOCK, (b + 1) * BLOCK
        blended = dot(weights[start:stop, :stop], values[:stop], ROWS_BY_COLUMNS) * inverse[start:stop]
        keep(0, b, jnp.where(alive(start), blended, 0.0))
    own = [give(0)]

    for b in reversed(range(blocks)):
        start, stop = b * BLOCK, (b + 1) * BLOCK
        block_weights = weights[start:stop, :stop]
        scale = inverse[start:stop]
        incoming = jnp.where(alive(start), given[start:stop].astype(jnp.float32), 0.0)
        row_dots = jnp.sum(incoming * results[0, chunks(b)].reshape(BLOCK, DIM).astype(jnp.float32), axis=1, keepdims=True)
        dweights = dot(incoming.astype(jnp.bfloat16), values[:stop], ROWS_BY_ROWS)
        dscores = (block_weights.astype(jnp.float32) * (dweights - row_dots)).astype(jnp.bfloat16)
        query_term = dot(dscores, keys[:stop], ROWS_BY_COLUMNS) * (scale * SCALE)
        keep(1, b, query_term)
        scaled_queries = (queries[start:stop].astype(jnp.float32) * scale).T.astype(jnp.bfloat16)
        scaled_incoming = (incoming * scale).T.astype(jnp.bfloat16)
        key_term = dot(scaled_queries, dscores, ROWS_BY_COLUMNS)
        value_term = dot(scaled_incoming, block_weights, ROWS_BY_COLUMNS)
        if b == blocks - 1:
            key_sum[:, :stop] = key_term
            value_sum[:, :stop] = value_term
        else:
            key_sum[:, :stop] += key_term
            value_sum[:, :stop] += value_term
        keep(2, b, (key_sum[:, start:stop] * SCALE).T)
        keep(3, b, value_sum[:, start:stop].T)

    own += [give(1), give(2), give(3)]
    for a in range(4):
        own[a].wait()
        wait_all(outs[a].at[:, pl.ds(0, (N - 1) * DIM)], send_out.at[a], recv_out.at[a])


def per_device(queries_in, keys_in, values_in, upstream, lengths, assignment, span_order):
    flat = [x.reshape(N // 2, 2 * SPAN, FEAT) for x in (keys_in, queries_in, values_in)]
    smem = pl.BlockSpec(memory_space=pltpu.SMEM)
    anywhere = pl.BlockSpec(memory_space=pl.ANY)
    bf16, f32 = jnp.bfloat16, jnp.float32
    results = pl.pallas_call(
        kernel,
        out_shape=[jax.ShapeDtypeStruct((ROWS, FEAT), bf16)] * 4,
        in_specs=[smem] * 3 + [anywhere] * 4,
        out_specs=[anywhere] * 4,
        scratch_shapes=[
            pltpu.SMEM((N,), jnp.int32),
            pltpu.VMEM((N // 2, 2 * SPAN, FEAT), bf16),
            pltpu.VMEM((N // 2, 2 * SPAN, FEAT), bf16),
            pltpu.VMEM((N // 2, 2 * SPAN, FEAT), bf16),
            pltpu.VMEM((3, N, ROWS, DIM), bf16),
            pltpu.VMEM((3, N, ROWS, DIM), bf16),
            pltpu.VMEM((3, N, 2, CHUNK, DIM), bf16),
            pltpu.VMEM((N, 2, CHUNK, DIM), bf16),
            pltpu.VMEM((N, 2, CHUNK, DIM), bf16),
            pltpu.VMEM((N, 2, CHUNK, DIM), bf16),
            pltpu.VMEM((N, 2, CHUNK, DIM), bf16),
            pltpu.VMEM((4, LEN, DIM), bf16),
            pltpu.VMEM((LEN, LEN), bf16),
            pltpu.VMEM((LEN, 1), f32),
            pltpu.VMEM((DIM, LEN), f32),
            pltpu.VMEM((DIM, LEN), f32),
            pltpu.VMEM((4, LEN // CHUNK, CHUNK, DIM), bf16),
            pltpu.VMEM((4, N, ROWS, DIM), bf16),
            pltpu.SemaphoreType.DMA((3,)),
            pltpu.SemaphoreType.DMA,
            pltpu.SemaphoreType.DMA((3,)),
            pltpu.SemaphoreType.DMA((3,)),
            pltpu.SemaphoreType.DMA((4,)),
            pltpu.SemaphoreType.DMA((4,)),
            pltpu.SemaphoreType.DMA((4,)),
            pltpu.SemaphoreType.DMA((4,)),
            pltpu.SemaphoreType.DMA((4,)),
        ],
        compiler_params=pltpu.CompilerParams(
            collective_id=0, has_side_effects=True, vmem_limit_bytes=56 * 1024 * 1024
        ),
    )(assignment, lengths, span_order, *flat, upstream.reshape(2, CHUNK, FEAT))
    return tuple(x.reshape(1, ROWS, FEAT) for x in results)


def solution(mesh):
    split = P("dp", None, "ctx", None)
    rows = P("dp", "ctx", None)
    return jax.shard_map(
        per_device,
        mesh=mesh,
        in_specs=(split, split, split, rows, P(), P(), P()),
        out_specs=(rows,) * 4,
        check_vma=False,
    )
```

time: 405 us -> 91.9 us (0.23)
  matrix products: 120 us -> 0 us
  waiting for transfers between devices: 106 us -> 0 us
  blocking collectives: 104 us -> 0 us
  Pallas kernels: 0 us -> 85.6 us
  local copies, waits for them, and re-layouts: 41.7 us -> 5.19 us
  between operations: 15.9 us -> 0.65 us
  other arithmetic: 15 us -> 0 us
    dot_general x22 -> x0, matrix products: 120 us -> none  [the longest x16 52.2 us: query_block(): jnp.einsum('hqk,khd->qhd', dscores, block_keys, preferred_element_type=jn...]
    all_gather x4 -> x0, waiting for transfers between devices: 105 us -> none  [the longest x1 64.1 us: per_device(): lax.all_gather(values, 'ctx', axis=0, tiled=True)]
    pallas_call x0 -> x1, Pallas kernels: none -> 85.6 us  [per_device(): pl.pallas_call(kernel, out_shape=[jax.ShapeDtypeStruct((ROWS, FEAT), bf16...]
    all_to_all x3 -> x0, blocking collectives: 67.1 us -> none  [the longest x1 27.1 us: per_device(): lax.all_to_all(jnp.take(keys_in[0], sources, axis=0), 'dp', split_axis=0,...]
    all_gather x2 -> x0, blocking collectives: 36.7 us -> none  [the longest x1 18.6 us: per_device(): lax.all_gather(row_dots, 'ctx', axis=0, tiled=True)]
    dynamic_slice x34 -> x0, local copies, waits for them, and re-layouts: 27.3 us -> none  [the longest x32 26.1 us: query_block(): lax.dynamic_slice_in_dim(scores, block * row_count, row_count, 2)]
    reduce_sum x2 -> x0, other arithmetic: 9.5 us -> none  [the longest x1 8.68 us: per_device(): totals = jnp.sum(weights, axis=2)]
    reshape x4 -> x0, local copies, waits for them, and re-layouts: 4.12 us -> none  [the longest x1 1.23 us: per_device(): values = values.reshape(row_count, HEADS, HEAD_DIM)]
  transfers between devices with their start and end apart: 4 -> 0, of which waited for: 3 -> 0; matrix products, arithmetic and copies ran while one was open for 34% -> 0% of each run, Pallas kernels for 0% -> 0%
where the time goes in v1:
time: 91.9 us; the launch traced here: 91.4 us
  Pallas kernels  85.6 us (93%)
  local copies, waits for them, and re-layouts  5.19 us (6%)
    pallas_call x1, Pallas kernels, per_device(): pl.pallas_call(kernel, out_shape=[jax.ShapeDtypeStruct((ROWS, FEAT), bf16...  85.6 us
    unnamed x10, local copies, waits for them, and re-layouts  5.19 us

profile of v1, /device:TPU:1, one launch (start us, length us, event | category | flops | bytes accessed | tf_op | source)
XLA Modules:
  0.0 91.4 jit_solution(13995240885115866199)
XLA Ops:
  0.6 85.6 %shard_map.102 = (bf16[128,2048]{1,0:T(8,128)(2,1)}, bf16[128,2048]{1,0:T(8,128)(2,1)}, bf16[128,2048]{1,0:T(8,128)(2,1)}, bf16[128,2048]{1,0:T(8,128)(2,1)}) custom-call(s32[16]{0:T(128)} %assignment.1, s32[16]{0:T(128)} %lengths.1, s32[16,256]{1,0:T(8,128)} %span_order.1, bf16[8,16,2048]{2,1,0:T(8,128)(2,1)} %bitcast.12, bf16[8,16,2048]{2,1,0:T(8,128)(2,1)} %bitcast.13, ...), custom_call_target="tpu_custom_call" | custom-call | tf_op jit(solution)/shard_map/pallas_call | solution.py:276
  86.2 0.0 copy-start.2
  86.2 1.9 %copy.15 = bf16[1,128,2048]{2,1,0:T(8,128)(2,1)} copy(bf16[1,128,2048]{2,1,0:T(8,128)(2,1)} %bitcast.11) | data formatting | bytes 1048576
  88.2 0.0 copy-done.2
  88.2 0.0 copy-start.1
  88.2 0.8 copy.16
  89.0 0.4 copy-done.1
  89.4 0.0 copy-start
  89.4 0.8 copy.17
  90.2 0.4 copy-done
  90.6 0.8 copy.18
Async XLA Ops:
  86.2 2.0 %copy-start.2 = (bf16[128,2048]{1,0:T(8,128)(2,1)S(1)}, bf16[128,2048]{1,0:T(8,128)(2,1)}, u32[]{:S(2)}) copy-start(bf16[128,2048]{1,0:T(8,128)(2,1)} %get-tuple-element.9) | copy-start | bytes 1572868
  88.2 1.2 %copy-start.1 = (bf16[128,2048]{1,0:T(8,128)(2,1)S(1)}, bf16[128,2048]{1,0:T(8,128)(2,1)}, u32[]{:S(2)}) copy-start(bf16[128,2048]{1,0:T(8,128)(2,1)} %get-tuple-element.10) | copy-start | bytes 1572868
  89.4 1.2 %copy-start = (bf16[128,2048]{1,0:T(8,128)(2,1)S(1)}, bf16[128,2048]{1,0:T(8,128)(2,1)}, u32[]{:S(2)}) copy-start(bf16[128,2048]{1,0:T(8,128)(2,1)} %get-tuple-element.11) | copy-start | bytes 1572868

commit v2 on v1

--- a/solution.py
+++ b/solution.py
@@ -1,3 +1,4 @@
+import functools
 import math
 
 import jax
@@ -16,6 +17,9 @@
 SPAN = 8
 CHUNK = 64
 BLOCK = 512
+WINDOW = 2
+FORWARD = 3
+ORDER = ((0, 0), (1, 0), (2, 0), (0, 1), (1, 1), (2, 1))
 SCALE = 1.0 / math.sqrt(DIM)
 LOG2E = math.log2(math.e)
 MASKED = -1e30
@@ -38,7 +42,7 @@
     sources, held_k, held_q, held_v, staged, landed, regrouped, arrived_k, arrived_q, arrived_v, arrived_g,
     ordered, weights, inverse,
     key_sum, value_sum, results, leaving,
-    held_sem, up_sem, send_one, recv_one, send_two, recv_two, send_out, recv_out, own_sem,
+    held_sem, up_sem, send_one, send_sibling, recv_one, send_two, recv_two, send_out, recv_out, own_sem,
 ):
     shard = lax.axis_index("dp")
     column = lax.axis_index("ctx")
@@ -99,24 +103,46 @@
         heads = [rows[:, h * DIM : (h + 1) * DIM] for h in range(N)]
         return jnp.concatenate(heads, axis=0).astype(jnp.bfloat16)
 
-    def first(a):
-        loads[a].wait()
-
-        def send(i, carry):
-            to = partner(shard, i)
+    core = lax.rem(shard, 2)
+    chip = lax.div(shard, 2)
+
+    def first(a, side):
+        def send(to, sem):
             staged[a, to] = by_head(a, to)
             pltpu.make_async_remote_copy(
                 src_ref=staged.at[a, to],
                 dst_ref=landed.at[a, shard],
-                send_sem=send_one.at[a],
+                send_sem=sem,
                 recv_sem=recv_one.at[a],
                 device_id=(to, column),
                 device_id_type=MESH,
             ).start()
-            return carry
-
-        lax.fori_loop(1, N, send, 0)
-        landed[a, shard] = by_head(a, shard)
+
+        def across(i, carry):
+            step = jnp.where(i % 2 == 1, (i + 1) // 2, N // 2 - i // 2)
+            send(2 * lax.rem(chip + step, N // 2) + side, send_one.at[side, a])
+            return carry
+
+        lax.fori_loop(1, N // 2, across, 0)
+
+        @pl.when(core == side)
+        def _():
+            landed[a, shard] = by_head(a, shard)
+
+        @pl.when(core != side)
+        def _():
+            send(2 * chip + side, send_sibling.at[a])
+
+    def sent(a, side):
+        some = staged.at[a, pl.ds(0, N // 2 - 1)]
+        pltpu.make_async_remote_copy(
+            src_ref=some,
+            dst_ref=some,
+            send_sem=send_one.at[side, a],
+            recv_sem=recv_one.at[a],
+            device_id=(shard, column),
+            device_id_type=MESH,
+        ).wait_send()
 
     def wait_all(buffer, send_sem, recv_sem):
         whole = pltpu.make_async_remote_copy(
@@ -131,7 +157,14 @@
         whole.wait_send()
 
     def second(a):
-        wait_all(landed.at[a, pl.ds(0, N - 1)], send_one.at[a], recv_one.at[a])
+        pltpu.make_async_remote_copy(
+            src_ref=staged.at[a, 0],
+            dst_ref=landed.at[a, pl.ds(0, N - 1)],
+            send_sem=send_sibling.at[a],
+            recv_sem=recv_one.at[a],
+            device_id=(shard, column),
+            device_id_type=MESH,
+        ).wait_recv()
 
         def regroup(pair, carry):
             both = landed[a, :, pl.ds(pl.multiple_of(pair * 16, 16), 16), :].astype(jnp.float32)
@@ -197,11 +230,18 @@
         own.start()
         return own
 
-    first(0)
-    first(1)
-    first(2)
-    second(0)
-    second(1)
+    for load in loads:
+        load.wait()
+    for i, (a, side) in enumerate(ORDER):
+        if i >= WINDOW:
+            sent(*ORDER[i - WINDOW])
+        first(a, side)
+        if i >= FORWARD:
+            pl.when(core == 0)(functools.partial(second, i - FORWARD))
+    for a in range(len(ORDER) - FORWARD, 3):
+        pl.when(core == 0)(functools.partial(second, a))
+    for a in range(3):
+        pl.when(core == 1)(functools.partial(second, a))
     own_up.wait()
     order(3)
     order(0)
@@ -209,7 +249,26 @@
 
     keys, queries, values, given = (ordered.at[a] for a in range(4))
     blocks = LEN // BLOCK
-    for b in range(blocks):
+
+    def chunks(b):
+        return slice(b * (BLOCK // CHUNK), (b + 1) * (BLOCK // CHUNK))
+
+    def keep(a, b, rows):
+        results[a, chunks(b)] = rows.astype(jnp.bfloat16).reshape(BLOCK // CHUNK, CHUNK, DIM)
+
+    def alive(start):
+        return start + lax.broadcasted_iota(jnp.int32, (BLOCK, 1), 0) < length
+
+    def incoming(b):
+        return jnp.where(alive(b * BLOCK), given[b * BLOCK : (b + 1) * BLOCK].astype(jnp.float32), 0.0)
+
+    def add(total, b, term):
+        if b == blocks - 1:
+            total[...] = term
+        else:
+            total[:, : (b + 1) * BLOCK] += term
+
+    for b in reversed(range(blocks)):
         start, stop = b * BLOCK, (b + 1) * BLOCK
         scores = dot(queries[start:stop], keys[:stop], ROWS_BY_ROWS)
         row = lax.broadcasted_iota(jnp.int32, (BLOCK, BLOCK), 0)
@@ -218,53 +277,54 @@
         scores = jnp.concatenate([scores[:, :start], last], axis=1) if b else last
         peak = jnp.max(scores, axis=1, keepdims=True)
         block_weights = jnp.exp2((scores - peak) * (SCALE * LOG2E))
-        inverse[start:stop] = 1.0 / jnp.sum(block_weights, axis=1, keepdims=True)
-        weights[start:stop, :stop] = block_weights.astype(jnp.bfloat16)
-
-    second(2)
+        scale = 1.0 / jnp.sum(block_weights, axis=1, keepdims=True)
+        inverse[start:stop] = scale
+        rounded = block_weights.astype(jnp.bfloat16)
+        weights[start:stop, :stop] = rounded
+        scaled_incoming = (incoming(b) * scale).T.astype(jnp.bfloat16)
+        add(value_sum, b, dot(scaled_incoming, rounded, ROWS_BY_COLUMNS))
+        keep(3, b, value_sum[:, start:stop].T)
+    own = [give(3)]
+
     order(2)
-
-    def chunks(b):
-        return slice(b * (BLOCK // CHUNK), (b + 1) * (BLOCK // CHUNK))
-
-    def keep(a, b, rows):
-        results[a, chunks(b)] = rows.astype(jnp.bfloat16).reshape(BLOCK // CHUNK, CHUNK, DIM)
-
-    def alive(start):
-        return start + lax.broadcasted_iota(jnp.int32, (BLOCK, 1), 0) < length
-
     for b in range(blocks):
         start, stop = b * BLOCK, (b + 1) * BLOCK
         blended = dot(weights[start:stop, :stop], values[:stop], ROWS_BY_COLUMNS) * inverse[start:stop]
         keep(0, b, jnp.where(alive(start), blended, 0.0))
-    own = [give(0)]
+    own.append(give(0))
 
     for b in reversed(range(blocks)):
         start, stop = b * BLOCK, (b + 1) * BLOCK
-        block_weights = weights[start:stop, :stop]
-        scale = inverse[start:stop]
-        incoming = jnp.where(alive(start), given[start:stop].astype(jnp.float32), 0.0)
-        row_dots = jnp.sum(incoming * results[0, chunks(b)].reshape(BLOCK, DIM).astype(jnp.float32), axis=1, keepdims=True)
-        dweights = dot(incoming.astype(jnp.bfloat16), values[:stop], ROWS_BY_ROWS)
-        dscores = (block_weights.astype(jnp.float32) * (dweights - row_dots)).astype(jnp.bfloat16)
-        query_term = dot(dscores, keys[:stop], ROWS_BY_COLUMNS) * (scale * SCALE)
-        keep(1, b, query_term)
-        scaled_queries = (queries[start:stop].astype(jnp.float32) * scale).T.astype(jnp.bfloat16)
-        scaled_incoming = (incoming * scale).T.astype(jnp.bfloat16)
-        key_term = dot(scaled_queries, dscores, ROWS_BY_COLUMNS)
-        value_term = dot(scaled_incoming, block_weights, ROWS_BY_COLUMNS)
-        if b == blocks - 1:
-            key_sum[:, :stop] = key_term
-            value_sum[:, :stop] = value_term
-        else:
-            key_sum[:, :stop] += key_term
-            value_sum[:, :stop] += value_term
+        block_incoming = incoming(b)
+        attended_rows = results[0, chunks(b)].reshape(BLOCK, DIM).astype(jnp.float32)
+        row_dots = jnp.sum(block_incoming * attended_rows, axis=1, keepdims=True)
+        dweights = dot(block_incoming.astype(jnp.bfloat16), values[:stop], ROWS_BY_ROWS)
+        dscores = (weights[start:stop, :stop].astype(jnp.float32) * (dweights - row_dots)).astype(jnp.bfloat16)
+        weights[start:stop, :stop] = dscores
+        keep(1, b, dot(dscores, keys[:stop], ROWS_BY_COLUMNS) * (inverse[start:stop] * SCALE))
+    own.append(give(1))
+
+    for b in reversed(range(blocks)):
+        start, stop = b * BLOCK, (b + 1) * BLOCK
+        scaled_queries = (queries[start:stop].astype(jnp.float32) * inverse[start:stop]).T.astype(jnp.bfloat16)
+        add(key_sum, b, dot(scaled_queries, weights[start:stop, :stop], ROWS_BY_COLUMNS))
         keep(2, b, (key_sum[:, start:stop] * SCALE).T)
-        keep(3, b, value_sum[:, start:stop].T)
-
-    own += [give(1), give(2), give(3)]
+    own.append(give(2))
+
+    for i in range(len(ORDER) - WINDOW, len(ORDER)):
+        sent(*ORDER[i])
+    for a in range(3):
+        pltpu.make_async_remote_copy(
+            src_ref=staged.at[a, 0],
+            dst_ref=staged.at[a, 0],
+            send_sem=send_sibling.at[a],
+            recv_sem=recv_one.at[a],
+            device_id=(shard, column),
+            device_id_type=MESH,
+        ).wait_send()
+    for copy in own:
+        copy.wait()
     for a in range(4):
-        own[a].wait()
         wait_all(outs[a].at[:, pl.ds(0, (N - 1) * DIM)], send_out.at[a], recv_out.at[a])
 
 
@@ -275,9 +335,9 @@
     bf16, f32 = jnp.bfloat16, jnp.float32
     results = pl.pallas_call(
         kernel,
-        out_shape=[jax.ShapeDtypeStruct((ROWS, FEAT), bf16)] * 4,
+        out_shape=[pltpu.VMEM((ROWS, FEAT), bf16)] * 4,
         in_specs=[smem] * 3 + [anywhere] * 4,
-        out_specs=[anywhere] * 4,
+        out_specs=[pl.BlockSpec(memory_space=pltpu.VMEM)] * 4,
         scratch_shapes=[
             pltpu.SMEM((N,), jnp.int32),
             pltpu.VMEM((N // 2, 2 * SPAN, FEAT), bf16),
@@ -299,6 +359,7 @@
             pltpu.VMEM((4, N, ROWS, DIM), bf16),
             pltpu.SemaphoreType.DMA((3,)),
             pltpu.SemaphoreType.DMA,
+            pltpu.SemaphoreType.DMA((2, 3)),
             pltpu.SemaphoreType.DMA((3,)),
             pltpu.SemaphoreType.DMA((3,)),
             pltpu.SemaphoreType.DMA((4,)),
@@ -308,7 +369,7 @@
             pltpu.SemaphoreType.DMA((4,)),
         ],
         compiler_params=pltpu.CompilerParams(
-            collective_id=0, has_side_effects=True, vmem_limit_bytes=56 * 1024 * 1024
+            collective_id=0, has_side_effects=True, vmem_limit_bytes=52 * 1024 * 1024
         ),
     )(assignment, lengths, span_order, *flat, upstream.reshape(2, CHUNK, FEAT))
     return tuple(x.reshape(1, ROWS, FEAT) for x in results)

time: 91.9 us -> 79.3 us (0.86)
  Pallas kernels: 85.6 us -> 75.3 us
  local copies, waits for them, and re-layouts: 5.19 us -> 3.17 us
    pallas_call x1, Pallas kernels: 85.6 us -> 75.3 us  [per_device(): pl.pallas_call(kernel, out_shape=[pltpu.VMEM((ROWS, FEAT), bf16)] * 4, in...]
    unnamed x10 -> x4, local copies, waits for them, and re-layouts: 5.19 us -> 3.17 us
where the time goes in v2:
time: 79.3 us; the launch traced here: 79.1 us
  Pallas kernels  75.3 us (95%)
  local copies, waits for them, and re-layouts  3.17 us (4%)
    pallas_call x1, Pallas kernels, per_device(): pl.pallas_call(kernel, out_shape=[pltpu.VMEM((ROWS, FEAT), bf16)] * 4, in...  75.3 us
    unnamed x4, local copies, waits for them, and re-layouts  3.17 us

profile of v2, /device:TPU:1, one launch (start us, length us, event | category | flops | bytes accessed | tf_op | source)
XLA Modules:
  0.0 79.1 jit_solution(11262569021652932931)
XLA Ops:
  0.6 75.3 %shard_map.102 = (bf16[128,2048]{1,0:T(8,128)(2,1)S(1)}, bf16[128,2048]{1,0:T(8,128)(2,1)S(1)}, bf16[128,2048]{1,0:T(8,128)(2,1)S(1)}, bf16[128,2048]{1,0:T(8,128)(2,1)S(1)}) custom-call(s32[16]{0:T(128)} %assignment.1, s32[16]{0:T(128)} %lengths.1, s32[16,256]{1,0:T(8,128)} %span_order.1, bf16[8,16,2048]{2,1,0:T(8,128)(2,1)} %bitcast.12, ...), custom_call_target="tpu_custom_call" | custom-call | tf_op jit(solution)/shard_map/pallas_call | solution.py:336
  76.0 0.8 %copy.15 = bf16[1,128,2048]{2,1,0:T(8,128)(2,1)} copy(bf16[1,128,2048]{2,1,0:T(8,128)(2,1)S(1)} %bitcast.11) | data formatting | bytes 1048576
  76.8 0.8 %copy.16 = bf16[1,128,2048]{2,1,0:T(8,128)(2,1)} copy(bf16[1,128,2048]{2,1,0:T(8,128)(2,1)S(1)} %bitcast.10) | data formatting | bytes 1048576
  77.6 0.8 %copy.17 = bf16[1,128,2048]{2,1,0:T(8,128)(2,1)} copy(bf16[1,128,2048]{2,1,0:T(8,128)(2,1)S(1)} %bitcast.9) | data formatting | bytes 1048576
  78.4 0.8 %copy.18 = bf16[1,128,2048]{2,1,0:T(8,128)(2,1)} copy(bf16[1,128,2048]{2,1,0:T(8,128)(2,1)S(1)} %bitcast.8) | data formatting | bytes 1048576

commit v3 on v2

--- a/solution.py
+++ b/solution.py
@@ -1,4 +1,3 @@
-import functools
 import math
 
 import jax
@@ -17,9 +16,10 @@
 SPAN = 8
 CHUNK = 64
 BLOCK = 512
-WINDOW = 2
-FORWARD = 3
-ORDER = ((0, 0), (1, 0), (2, 0), (0, 1), (1, 1), (2, 1))
+PLAN = (
+    (1, 0, 0), (1, 1, 0), (2, 0, 0), (1, 2, 0), (2, 1, 0), (1, 0, 1), (2, 2, 0),
+    (1, 1, 1), (1, 3, 0), (2, 0, 1), (1, 2, 1), (2, 1, 1), (2, 2, 1),
+)
 SCALE = 1.0 / math.sqrt(DIM)
 LOG2E = math.log2(math.e)
 MASKED = -1e30
@@ -39,10 +39,10 @@
 def kernel(
     assignment, lengths, span_order, keys_in, queries_in, values_in, upstream,
     attended, query_grad, key_grad, value_grad,
-    sources, held_k, held_q, held_v, staged, landed, regrouped, arrived_k, arrived_q, arrived_v, arrived_g,
+    sources, held_k, held_q, held_v, packed, landed, staged, arrived_k, arrived_q, arrived_v, arrived_g, pieces,
     ordered, weights, inverse,
     key_sum, value_sum, results, leaving,
-    held_sem, up_sem, send_one, send_sibling, recv_one, send_two, recv_two, send_out, recv_out, own_sem,
+    held_sem, up_sem, send_x, recv_x, send_z, send_sibling, recv_z, send_up, recv_up, send_out, recv_out, own_sem,
 ):
     shard = lax.axis_index("dp")
     column = lax.axis_index("ctx")
@@ -82,67 +82,47 @@
         pltpu.make_async_remote_copy(
             src_ref=upstream.at[:, :, pl.ds(pl.multiple_of(to * DIM, DIM), DIM)],
             dst_ref=arrived[3].at[column],
-            send_sem=send_two.at[3],
-            recv_sem=recv_two.at[3],
+            send_sem=send_up,
+            recv_sem=recv_up,
             device_id=(shard, to),
             device_id_type=MESH,
         ).start()
         return carry
 
-    lax.fori_loop(1, N, send_upstream, 0)
     own_up = pltpu.make_async_copy(
         upstream.at[:, :, pl.ds(pl.multiple_of(column * DIM, DIM), DIM)], arrived[3].at[column], up_sem
     )
     own_up.start()
 
-    def by_head(a, to):
+    core = lax.rem(shard, 2)
+    chip = lax.div(shard, 2)
+
+    def rows_of(a, to):
         e = sources[to]
         pair = held[a][lax.div(e, 2)].astype(jnp.float32)
         odd = jnp.full((SPAN, FEAT), lax.rem(e, 2), jnp.int32) == 1
-        rows = jnp.where(odd, pair[SPAN:], pair[:SPAN])
-        heads = [rows[:, h * DIM : (h + 1) * DIM] for h in range(N)]
-        return jnp.concatenate(heads, axis=0).astype(jnp.bfloat16)
-
-    core = lax.rem(shard, 2)
-    chip = lax.div(shard, 2)
+        return jnp.where(odd, pair[SPAN:], pair[:SPAN])
 
     def first(a, side):
-        def send(to, sem):
-            staged[a, to] = by_head(a, to)
+        for q in range(N // 4):
+            both = jnp.concatenate([rows_of(a, 4 * q + side), rows_of(a, 4 * q + 2 + side)], axis=0).astype(jnp.bfloat16)
+            for h in range(N):
+                packed[a, side, h, 16 * q : 16 * q + 16] = both[:, h * DIM : (h + 1) * DIM]
+
+        def send(i, carry):
+            to = partner(column, i)
             pltpu.make_async_remote_copy(
-                src_ref=staged.at[a, to],
-                dst_ref=landed.at[a, shard],
-                send_sem=sem,
-                recv_sem=recv_one.at[a],
-                device_id=(to, column),
+                src_ref=packed.at[a, side, to],
+                dst_ref=landed.at[a, side, column],
+                send_sem=send_x.at[side, a],
+                recv_sem=recv_x.at[side, a],
+                device_id=(shard, to),
                 device_id_type=MESH,
             ).start()
-
-        def across(i, carry):
-            step = jnp.where(i % 2 == 1, (i + 1) // 2, N // 2 - i // 2)
-            send(2 * lax.rem(chip + step, N // 2) + side, send_one.at[side, a])
             return carry
 
-        lax.fori_loop(1, N // 2, across, 0)
-
-        @pl.when(core == side)
-        def _():
-            landed[a, shard] = by_head(a, shard)
-
-        @pl.when(core != side)
-        def _():
-            send(2 * chip + side, send_sibling.at[a])
-
-    def sent(a, side):
-        some = staged.at[a, pl.ds(0, N // 2 - 1)]
-        pltpu.make_async_remote_copy(
-            src_ref=some,
-            dst_ref=some,
-            send_sem=send_one.at[side, a],
-            recv_sem=recv_one.at[a],
-            device_id=(shard, column),
-            device_id_type=MESH,
-        ).wait_send()
+        lax.fori_loop(1, N, send, 0)
+        landed[a, side, column] = packed[a, side, column]
 
     def wait_all(buffer, send_sem, recv_sem):
         whole = pltpu.make_async_remote_copy(
@@ -156,61 +136,81 @@
         whole.wait_recv()
         whole.wait_send()
 
-    def second(a):
-        pltpu.make_async_remote_copy(
-            src_ref=staged.at[a, 0],
-            dst_ref=landed.at[a, pl.ds(0, N - 1)],
-            send_sem=send_sibling.at[a],
-            recv_sem=recv_one.at[a],
+    def second(a, side):
+        wait_all(landed.at[a, side, pl.ds(0, N - 1)], send_x.at[side, a], recv_x.at[side, a])
+        for q in range(N // 4):
+            both = landed[a, side, :, 16 * q : 16 * q + 16].astype(jnp.float32)
+            staged[a, 4 * q + side] = both[:, :SPAN].reshape(ROWS, DIM).astype(jnp.bfloat16)
+            staged[a, 4 * q + 2 + side] = both[:, SPAN:].reshape(ROWS, DIM).astype(jnp.bfloat16)
+
+        def send(to, sem):
+            pltpu.make_async_remote_copy(
+                src_ref=staged.at[a, to],
+                dst_ref=arrived[a].at[shard],
+                send_sem=sem,
+                recv_sem=recv_z.at[a],
+                device_id=(to, column),
+                device_id_type=MESH,
+            ).start()
+
+        def across(i, carry):
+            step = jnp.where(i % 2 == 1, (i + 1) // 2, N // 2 - i // 2)
+            send(2 * lax.rem(chip + step, N // 2) + side, send_z.at[side, a])
+            return carry
+
+        lax.fori_loop(1, N // 2, across, 0)
+
+        @pl.when(core == side)
+        def _():
+            arrived[a][shard] = staged[a, shard]
+
+        @pl.when(core != side)
+        def _():
+            send(2 * chip + side, send_sibling.at[a])
+
+    def one_way(source, target, send_sem, recv_sem):
+        return pltpu.make_async_remote_copy(
+            src_ref=source,
+            dst_ref=target,
+            send_sem=send_sem,
+            recv_sem=recv_sem,
             device_id=(shard, column),
             device_id_type=MESH,
-        ).wait_recv()
-
-        def regroup(pair, carry):
-            both = landed[a, :, pl.ds(pl.multiple_of(pair * 16, 16), 16), :].astype(jnp.float32)
-            regrouped[a, 2 * pair] = both[:, :SPAN].reshape(2, CHUNK, DIM).astype(jnp.bfloat16)
-            regrouped[a, 2 * pair + 1] = both[:, SPAN:].reshape(2, CHUNK, DIM).astype(jnp.bfloat16)
-            return carry
-
-        lax.fori_loop(0, N // 2, regroup, 0)
-
-        def send(i, carry):
-            to = partner(column, i)
-            pltpu.make_async_remote_copy(
-                src_ref=regrouped.at[a, to],
-                dst_ref=arrived[a].at[column],
-                send_sem=send_two.at[a],
-                recv_sem=recv_two.at[a],
-                device_id=(shard, to),
-                device_id_type=MESH,
-            ).start()
-            return carry
-
-        lax.fori_loop(1, N, send, 0)
-        arrived[a][column] = regrouped[a, column]
-
-    def order(a):
-        wait_all(arrived[a].at[pl.ds(0, N - 1)], send_two.at[a], recv_two.at[a])
-
-        def place(p, carry):
+        )
+
+    def sent(a):
+        some = staged.at[a, pl.ds(0, N // 2 - 1)]
+        for side in range(2):
+            one_way(some, some, send_z.at[side, a], recv_z.at[a]).wait_send()
+        one_way(staged.at[a, 0], staged.at[a, 0], send_sibling.at[a], recv_z.at[a]).wait_send()
+
+    def sort(a, source):
+        for p in range(2 * N):
             second_half = p // N
             piece = p // 2 + folded * (p + second_half * (2 * N - 1 - 2 * p) - p // 2)
             half = p % 2 + folded * (second_half - p % 2)
-            ordered[a, pl.ds(pl.multiple_of(p * CHUNK, CHUNK), CHUNK), :] = arrived[a][piece, half]
-            return carry
-
-        lax.fori_loop(0, 2 * N, place, 0)
+            ordered[a, p * CHUNK : (p + 1) * CHUNK] = source[piece, half]
+
+    def order(a):
+        if a == 3:
+            own_up.wait()
+            wait_all(arrived[3].at[pl.ds(0, N - 1)], send_up, recv_up)
+            sort(3, arrived[3])
+            return
+        some = arrived[a].at[pl.ds(0, N - 1)]
+        one_way(some, some, send_z.at[0, a], recv_z.at[a]).wait_recv()
+        for c in range(0, N, 2):
+            both = arrived[a][:, c * SPAN : (c + 2) * SPAN].astype(jnp.float32)
+            pieces[c] = both[:, :SPAN].reshape(2, CHUNK, DIM).astype(jnp.bfloat16)
+            pieces[c + 1] = both[:, SPAN:].reshape(2, CHUNK, DIM).astype(jnp.bfloat16)
+        sort(a, pieces)
 
     def give(a):
-        def send(i, carry):
-            to = partner(column, i)
+        for to in range(N):
             low = 2 * to - folded * to
             high = 2 * to + 1 + folded * (2 * N - 2 - 3 * to)
             leaving[a, to, :CHUNK] = results[a, low]
             leaving[a, to, CHUNK:] = results[a, high]
-            return carry
-
-        lax.fori_loop(0, N, send, 0)
         own_columns = pl.ds(pl.multiple_of(column * DIM, DIM), DIM)
 
         def start(i, carry):
@@ -232,20 +232,16 @@
 
     for load in loads:
         load.wait()
-    for i, (a, side) in enumerate(ORDER):
-        if i >= WINDOW:
-            sent(*ORDER[i - WINDOW])
-        first(a, side)
-        if i >= FORWARD:
-            pl.when(core == 0)(functools.partial(second, i - FORWARD))
-    for a in range(len(ORDER) - FORWARD, 3):
-        pl.when(core == 0)(functools.partial(second, a))
-    for a in range(3):
-        pl.when(core == 1)(functools.partial(second, a))
-    own_up.wait()
-    order(3)
+    for todo, a, side in PLAN:
+        if todo == 2:
+            second(a, side)
+        elif a < 3:
+            first(a, side)
+        else:
+            lax.fori_loop(1, N, send_upstream, 0)
     order(0)
     order(1)
+    order(3)
 
     keys, queries, values, given = (ordered.at[a] for a in range(4))
     blocks = LEN // BLOCK
@@ -277,12 +273,14 @@
         scores = jnp.concatenate([scores[:, :start], last], axis=1) if b else last
         peak = jnp.max(scores, axis=1, keepdims=True)
         block_weights = jnp.exp2((scores - peak) * (SCALE * LOG2E))
-        scale = 1.0 / jnp.sum(block_weights, axis=1, keepdims=True)
-        inverse[start:stop] = scale
+        inverse[start:stop] = 1.0 / jnp.sum(block_weights, axis=1, keepdims=True)
         rounded = block_weights.astype(jnp.bfloat16)
         weights[start:stop, :stop] = rounded
-        scaled_incoming = (incoming(b) * scale).T.astype(jnp.bfloat16)
-        add(value_sum, b, dot(scaled_incoming, rounded, ROWS_BY_COLUMNS))
+
+    for b in reversed(range(blocks)):
+        start, stop = b * BLOCK, (b + 1) * BLOCK
+        scaled_incoming = (incoming(b) * inverse[start:stop]).T.astype(jnp.bfloat16)
+        add(value_sum, b, dot(scaled_incoming, weights[start:stop, :stop], ROWS_BY_COLUMNS))
         keep(3, b, value_sum[:, start:stop].T)
     own = [give(3)]
 
@@ -311,17 +309,8 @@
         keep(2, b, (key_sum[:, start:stop] * SCALE).T)
     own.append(give(2))
 
-    for i in range(len(ORDER) - WINDOW, len(ORDER)):
-        sent(*ORDER[i])
     for a in range(3):
-        pltpu.make_async_remote_copy(
-            src_ref=staged.at[a, 0],
-            dst_ref=staged.at[a, 0],
-            send_sem=send_sibling.at[a],
-            recv_sem=recv_one.at[a],
-            device_id=(shard, column),
-            device_id_type=MESH,
-        ).wait_send()
+        sent(a)
     for copy in own:
         copy.wait()
     for a in range(4):
@@ -343,11 +332,12 @@
             pltpu.VMEM((N // 2, 2 * SPAN, FEAT), bf16),
             pltpu.VMEM((N // 2, 2 * SPAN, FEAT), bf16),
             pltpu.VMEM((N // 2, 2 * SPAN, FEAT), bf16),
+            pltpu.VMEM((3, 2, N, CHUNK, DIM), bf16),
+            pltpu.VMEM((3, 2, N, CHUNK, DIM), bf16),
             pltpu.VMEM((3, N, ROWS, DIM), bf16),
-            pltpu.VMEM((3, N, ROWS, DIM), bf16),
-            pltpu.VMEM((3, N, 2, CHUNK, DIM), bf16),
-            pltpu.VMEM((N, 2, CHUNK, DIM), bf16),
-            pltpu.VMEM((N, 2, CHUNK, DIM), bf16),
+            pltpu.VMEM((N, ROWS, DIM), bf16),
+            pltpu.VMEM((N, ROWS, DIM), bf16),
+            pltpu.VMEM((N, ROWS, DIM), bf16),
             pltpu.VMEM((N, 2, CHUNK, DIM), bf16),
             pltpu.VMEM((N, 2, CHUNK, DIM), bf16),
             pltpu.VMEM((4, LEN, DIM), bf16),
@@ -360,10 +350,12 @@
             pltpu.SemaphoreType.DMA((3,)),
             pltpu.SemaphoreType.DMA,
             pltpu.SemaphoreType.DMA((2, 3)),
+            pltpu.SemaphoreType.DMA((2, 3)),
+            pltpu.SemaphoreType.DMA((2, 3)),
             pltpu.SemaphoreType.DMA((3,)),
             pltpu.SemaphoreType.DMA((3,)),
-            pltpu.SemaphoreType.DMA((4,)),
-            pltpu.SemaphoreType.DMA((4,)),
+            pltpu.SemaphoreType.DMA,
+            pltpu.SemaphoreType.DMA,
             pltpu.SemaphoreType.DMA((4,)),
             pltpu.SemaphoreType.DMA((4,)),
             pltpu.SemaphoreType.DMA((4,)),

time: 79.3 us -> 75.4 us (0.951)
  Pallas kernels: 75.3 us -> 71.5 us
    pallas_call x1, Pallas kernels: 75.3 us -> 71.5 us  [per_device(): pl.pallas_call(kernel, out_shape=[pltpu.VMEM((ROWS, FEAT), bf16)] * 4, in...]
where the time goes in v3:
time: 75.4 us; the launch traced here: 75.3 us
  Pallas kernels  71.5 us (95%)
  local copies, waits for them, and re-layouts  3.17 us (4%)
    pallas_call x1, Pallas kernels, per_device(): pl.pallas_call(kernel, out_shape=[pltpu.VMEM((ROWS, FEAT), bf16)] * 4, in...  71.5 us
    unnamed x4, local copies, waits for them, and re-layouts  3.17 us

profile of v3, /device:TPU:1, one launch (start us, length us, event | category | flops | bytes accessed | tf_op | source)
XLA Modules:
  0.0 75.3 jit_solution(9483105860799761606)
XLA Ops:
  0.6 71.5 %shard_map.102 = (bf16[128,2048]{1,0:T(8,128)(2,1)S(1)}, bf16[128,2048]{1,0:T(8,128)(2,1)S(1)}, bf16[128,2048]{1,0:T(8,128)(2,1)S(1)}, bf16[128,2048]{1,0:T(8,128)(2,1)S(1)}) custom-call(s32[16]{0:T(128)} %assignment.1, s32[16]{0:T(128)} %lengths.1, s32[16,256]{1,0:T(8,128)} %span_order.1, bf16[8,16,2048]{2,1,0:T(8,128)(2,1)} %bitcast.12, ...), custom_call_target="tpu_custom_call" | custom-call | tf_op jit(solution)/shard_map/pallas_call | solution.py:325
  72.1 0.8 %copy.15 = bf16[1,128,2048]{2,1,0:T(8,128)(2,1)} copy(bf16[1,128,2048]{2,1,0:T(8,128)(2,1)S(1)} %bitcast.11) | data formatting | bytes 1048576
  72.9 0.8 %copy.16 = bf16[1,128,2048]{2,1,0:T(8,128)(2,1)} copy(bf16[1,128,2048]{2,1,0:T(8,128)(2,1)S(1)} %bitcast.10) | data formatting | bytes 1048576
  73.7 0.8 %copy.17 = bf16[1,128,2048]{2,1,0:T(8,128)(2,1)} copy(bf16[1,128,2048]{2,1,0:T(8,128)(2,1)S(1)} %bitcast.9) | data formatting | bytes 1048576
  74.5 0.8 %copy.18 = bf16[1,128,2048]{2,1,0:T(8,128)(2,1)} copy(bf16[1,128,2048]{2,1,0:T(8,128)(2,1)S(1)} %bitcast.8) | data formatting | bytes 1048576

commit v4 on v3

--- a/solution.py
+++ b/solution.py
@@ -15,7 +15,9 @@
 FEAT = 2048
 SPAN = 8
 CHUNK = 64
-BLOCK = 512
+SCORE_BLOCK = 256
+QUERY_BLOCK = 512
+VALUE_BLOCK = 512
 PLAN = (
     (1, 0, 0), (1, 1, 0), (2, 0, 0), (1, 2, 0), (2, 1, 0), (1, 0, 1), (2, 2, 0),
     (1, 1, 1), (1, 3, 0), (2, 0, 1), (1, 2, 1), (2, 1, 1), (2, 2, 1),
@@ -244,69 +246,67 @@
     order(3)
 
     keys, queries, values, given = (ordered.at[a] for a in range(4))
-    blocks = LEN // BLOCK
-
-    def chunks(b):
-        return slice(b * (BLOCK // CHUNK), (b + 1) * (BLOCK // CHUNK))
-
-    def keep(a, b, rows):
-        results[a, chunks(b)] = rows.astype(jnp.bfloat16).reshape(BLOCK // CHUNK, CHUNK, DIM)
-
-    def alive(start):
-        return start + lax.broadcasted_iota(jnp.int32, (BLOCK, 1), 0) < length
-
-    def incoming(b):
-        return jnp.where(alive(b * BLOCK), given[b * BLOCK : (b + 1) * BLOCK].astype(jnp.float32), 0.0)
-
-    def add(total, b, term):
-        if b == blocks - 1:
+
+    def spans(size):
+        return [(start, start + size) for start in reversed(range(0, LEN, size))]
+
+    def keep(a, start, rows):
+        some = rows.shape[0] // CHUNK
+        results[a, start // CHUNK : start // CHUNK + some] = rows.astype(jnp.bfloat16).reshape(some, CHUNK, DIM)
+
+    def alive(start, stop):
+        return start + lax.broadcasted_iota(jnp.int32, (stop - start, 1), 0) < length
+
+    def incoming(start, stop):
+        return jnp.where(alive(start, stop), given[start:stop].astype(jnp.float32), 0.0)
+
+    def add(total, stop, term):
+        if stop == LEN:
             total[...] = term
         else:
-            total[:, : (b + 1) * BLOCK] += term
-
-    for b in reversed(range(blocks)):
-        start, stop = b * BLOCK, (b + 1) * BLOCK
+            total[:, :stop] += term
+
+    for start, stop in spans(SCORE_BLOCK):
         scores = dot(queries[start:stop], keys[:stop], ROWS_BY_ROWS)
-        row = lax.broadcasted_iota(jnp.int32, (BLOCK, BLOCK), 0)
-        col = lax.broadcasted_iota(jnp.int32, (BLOCK, BLOCK), 1)
+        row = lax.broadcasted_iota(jnp.int32, (SCORE_BLOCK, SCORE_BLOCK), 0)
+        col = lax.broadcasted_iota(jnp.int32, (SCORE_BLOCK, SCORE_BLOCK), 1)
         last = jnp.where(col <= row, scores[:, start:], MASKED)
-        scores = jnp.concatenate([scores[:, :start], last], axis=1) if b else last
+        scores = jnp.concatenate([scores[:, :start], last], axis=1) if start else last
         peak = jnp.max(scores, axis=1, keepdims=True)
         block_weights = jnp.exp2((scores - peak) * (SCALE * LOG2E))
         inverse[start:stop] = 1.0 / jnp.sum(block_weights, axis=1, keepdims=True)
-        rounded = block_weights.astype(jnp.bfloat16)
-        weights[start:stop, :stop] = rounded
-
-    for b in reversed(range(blocks)):
-        start, stop = b * BLOCK, (b + 1) * BLOCK
-        scaled_incoming = (incoming(b) * inverse[start:stop]).T.astype(jnp.bfloat16)
-        add(value_sum, b, dot(scaled_incoming, weights[start:stop, :stop], ROWS_BY_COLUMNS))
-        keep(3, b, value_sum[:, start:stop].T)
+        weights[start:stop, :stop] = block_weights.astype(jnp.bfloat16)
+        if SCORE_BLOCK < VALUE_BLOCK and start % VALUE_BLOCK + SCORE_BLOCK < VALUE_BLOCK:
+            weights[start:stop, stop : start - start % VALUE_BLOCK + VALUE_BLOCK] = jnp.zeros(
+                (SCORE_BLOCK, VALUE_BLOCK - start % VALUE_BLOCK - SCORE_BLOCK), jnp.bfloat16
+            )
+
+    for start, stop in spans(VALUE_BLOCK):
+        scaled_incoming = (incoming(start, stop) * inverse[start:stop]).T.astype(jnp.bfloat16)
+        add(value_sum, stop, dot(scaled_incoming, weights[start:stop, :stop], ROWS_BY_COLUMNS))
+        keep(3, start, value_sum[:, start:stop].T)
     own = [give(3)]
 
     order(2)
-    for b in range(blocks):
-        start, stop = b * BLOCK, (b + 1) * BLOCK
+    for start, stop in spans(VALUE_BLOCK):
         blended = dot(weights[start:stop, :stop], values[:stop], ROWS_BY_COLUMNS) * inverse[start:stop]
-        keep(0, b, jnp.where(alive(start), blended, 0.0))
+        keep(0, start, jnp.where(alive(start, stop), blended, 0.0))
     own.append(give(0))
 
-    for b in reversed(range(blocks)):
-        start, stop = b * BLOCK, (b + 1) * BLOCK
-        block_incoming = incoming(b)
-        attended_rows = results[0, chunks(b)].reshape(BLOCK, DIM).astype(jnp.float32)
+    for start, stop in spans(QUERY_BLOCK):
+        block_incoming = incoming(start, stop)
+        attended_rows = results[0, start // CHUNK : stop // CHUNK].reshape(QUERY_BLOCK, DIM).astype(jnp.float32)
         row_dots = jnp.sum(block_incoming * attended_rows, axis=1, keepdims=True)
         dweights = dot(block_incoming.astype(jnp.bfloat16), values[:stop], ROWS_BY_ROWS)
         dscores = (weights[start:stop, :stop].astype(jnp.float32) * (dweights - row_dots)).astype(jnp.bfloat16)
         weights[start:stop, :stop] = dscores
-        keep(1, b, dot(dscores, keys[:stop], ROWS_BY_COLUMNS) * (inverse[start:stop] * SCALE))
+        keep(1, start, dot(dscores, keys[:stop], ROWS_BY_COLUMNS) * (inverse[start:stop] * SCALE))
     own.append(give(1))
 
-    for b in reversed(range(blocks)):
-        start, stop = b * BLOCK, (b + 1) * BLOCK
+    for start, stop in spans(VALUE_BLOCK):
         scaled_queries = (queries[start:stop].astype(jnp.float32) * inverse[start:stop]).T.astype(jnp.bfloat16)
-        add(key_sum, b, dot(scaled_queries, weights[start:stop, :stop], ROWS_BY_COLUMNS))
-        keep(2, b, (key_sum[:, start:stop] * SCALE).T)
+        add(key_sum, stop, dot(scaled_queries, weights[start:stop, :stop], ROWS_BY_COLUMNS))
+        keep(2, start, (key_sum[:, start:stop] * SCALE).T)
     own.append(give(2))
 
     for a in range(3):

time: 75.4 us -> 74.6 us (0.989)
  Pallas kernels: 71.5 us -> 70.6 us
    pallas_call x1, Pallas kernels: 71.5 us -> 70.6 us  [per_device(): pl.pallas_call(kernel, out_shape=[pltpu.VMEM((ROWS, FEAT), bf16)] * 4, in...]
where the time goes in v4:
time: 74.6 us; the launch traced here: 74.4 us
  Pallas kernels  70.6 us (95%)
  local copies, waits for them, and re-layouts  3.17 us (4%)
    pallas_call x1, Pallas kernels, per_device(): pl.pallas_call(kernel, out_shape=[pltpu.VMEM((ROWS, FEAT), bf16)] * 4, in...  70.6 us
    unnamed x4, local copies, waits for them, and re-layouts  3.17 us

profile of v4, /device:TPU:1, one launch (start us, length us, event | category | flops | bytes accessed | tf_op | source)
XLA Modules:
  0.0 74.4 jit_solution(17278978550540576421)
XLA Ops:
  0.6 70.6 %shard_map.102 = (bf16[128,2048]{1,0:T(8,128)(2,1)S(1)}, bf16[128,2048]{1,0:T(8,128)(2,1)S(1)}, bf16[128,2048]{1,0:T(8,128)(2,1)S(1)}, bf16[128,2048]{1,0:T(8,128)(2,1)S(1)}) custom-call(s32[16]{0:T(128)} %assignment.1, s32[16]{0:T(128)} %lengths.1, s32[16,256]{1,0:T(8,128)} %span_order.1, bf16[8,16,2048]{2,1,0:T(8,128)(2,1)} %bitcast.12, ...), custom_call_target="tpu_custom_call" | custom-call | tf_op jit(solution)/shard_map/pallas_call | solution.py:325
  71.2 0.8 %copy.15 = bf16[1,128,2048]{2,1,0:T(8,128)(2,1)} copy(bf16[1,128,2048]{2,1,0:T(8,128)(2,1)S(1)} %bitcast.11) | data formatting | bytes 1048576
  72.0 0.8 %copy.16 = bf16[1,128,2048]{2,1,0:T(8,128)(2,1)} copy(bf16[1,128,2048]{2,1,0:T(8,128)(2,1)S(1)} %bitcast.10) | data formatting | bytes 1048576
  72.8 0.8 %copy.17 = bf16[1,128,2048]{2,1,0:T(8,128)(2,1)} copy(bf16[1,128,2048]{2,1,0:T(8,128)(2,1)S(1)} %bitcast.9) | data formatting | bytes 1048576
  73.6 0.8 %copy.18 = bf16[1,128,2048]{2,1,0:T(8,128)(2,1)} copy(bf16[1,128,2048]{2,1,0:T(8,128)(2,1)S(1)} %bitcast.8) | data formatting | bytes 1048576
